TPU v7x, 32 devices: a whole 2x2x4 slice. The times are simulated.
32 devices in a mesh: dp: 8 (over z, x), fsdp: 4 (over y, core).
Axes of the slice: x: 2, y: 2, z: 4, core: 2. Of those that a mesh axis runs over, the one named last changes fastest.
Arguments:
- inputs: bfloat16 [16, 1024, 1024], P('dp', 'fsdp'), may hold values from -6 to 6
- segment_ids: int32 [16, 1024], P('dp', 'fsdp'), may hold values from 0 to 2, as said below
- cotangent: bfloat16 [16, 1024, 1024], P('dp', 'fsdp'), may hold values from -6 to 6
- ln1_gain: bfloat16 [1024], P(('dp', 'fsdp')), may hold values from 0.5 to 1.5
- ln1_bias: bfloat16 [1024], P(('dp', 'fsdp')), may hold values from -1.75 to 1.75
- w_qkv: bfloat16 [1024, 3072], P(('dp', 'fsdp')), may hold values from -0.1875 to 0.1875
- q_bias: bfloat16 [1024], P(('dp', 'fsdp')), may hold values from -3 to 3
- v_bias: bfloat16 [1024], P(('dp', 'fsdp')), may hold values from -3 to 3
- w_proj: bfloat16 [1024, 1024], P(('dp', 'fsdp')), may hold values from -2 to 2
- proj_bias: bfloat16 [1024], P(('dp', 'fsdp')), may hold values from -1.75 to 1.75
- ln2_gain: bfloat16 [1024], P(('dp', 'fsdp')), may hold values from 0.5 to 1.5
- ln2_bias: bfloat16 [1024], P(('dp', 'fsdp')), may hold values from -1.75 to 1.75
- w_fc: bfloat16 [1024, 4096], P(('dp', 'fsdp')), may hold values from -0.1875 to 0.1875
- fc_bias: bfloat16 [4096], P(('dp', 'fsdp')), may hold values from -3 to 3
- w_out: bfloat16 [4096, 1024], P(('dp', 'fsdp')), may hold values from -0.09375 to 0.09375
- out_bias: bfloat16 [1024], P(('dp', 'fsdp')), may hold values from -1.75 to 1.75
Outputs:
- block_output: bfloat16 [16, 1024, 1024], P('dp', 'fsdp')
- input_grad: bfloat16 [16, 1024, 1024], P('dp', 'fsdp')
- ln1_gain_grad: float32 [1024], P(('dp', 'fsdp'))
- ln1_bias_grad: float32 [1024], P(('dp', 'fsdp'))
- w_qkv_grad: float32 [1024, 3072], P(('dp', 'fsdp'))
- q_bias_grad: float32 [1024], P(('dp', 'fsdp'))
- v_bias_grad: float32 [1024], P(('dp', 'fsdp'))
- w_proj_grad: float32 [1024, 1024], P(('dp', 'fsdp'))
- proj_bias_grad: float32 [1024], P(('dp', 'fsdp'))
- ln2_gain_grad: float32 [1024], P(('dp', 'fsdp'))
- ln2_bias_grad: float32 [1024], P(('dp', 'fsdp'))
- w_fc_grad: float32 [1024, 4096], P(('dp', 'fsdp'))
- fc_bias_grad: float32 [4096], P(('dp', 'fsdp'))
- w_out_grad: float32 [4096, 1024], P(('dp', 'fsdp'))
- out_bias_grad: float32 [1024], P(('dp', 'fsdp'))
Inputs may be any that keep to these rules, and one draw needn't show every extreme that they name: `segment_ids`: within each sequence the ids start at 0 and never fall; every sequence that holds several documents ends with document 2; among the 2 sequences of each dp index one is a single document.
All inputs are finite; a program needn't handle non-finite values.
Results may differ from a plain program's by a relative error of at most 0.013.
Values may be sent and summed in bfloat16 or wider, within the bound.
A program may use at most 192 MiB of HBM per device.

v0:
```python
import jax
import jax.numpy as jnp
from jax import lax
from jax.sharding import PartitionSpec as P

H = 16
HD = 64
MICRO = 2


def layer_norm(values, gain, shift):
    center = values - jnp.mean(values, axis=-1, keepdims=True)
    spread = jnp.mean(center * center, axis=-1, keepdims=True)
    return center * lax.rsqrt(spread + 1e-05) * gain + shift


def gelu_tanh(values):
    return jax.nn.gelu(values, approximate=True)


def row_dot(left, right):
    return jnp.dot(left, right, preferred_element_type=jnp.float32)


def col_dot(left, right):
    return lax.dot_general(
        left, right, (((0,), (0,)), ((), ())), preferred_element_type=jnp.float32
    )


def back_dot(left, right):
    return lax.dot_general(
        left, right, (((1,), (1,)), ((), ())), preferred_element_type=jnp.float32
    )


def score_block(queries, keys_all, allowed):
    raw = jnp.einsum(
        "qhd,khd->hqk",
        queries.reshape(-1, H, HD),
        keys_all.reshape(-1, H, HD),
        preferred_element_type=jnp.float32,
    ) * HD ** (-0.5)
    return jnp.where(allowed[None], raw, -1e30)


def attend_forward(item):
    queries, keys_all, values_all, allowed = item
    scores = score_block(queries, keys_all, allowed)
    top_score = jnp.max(scores, axis=-1, keepdims=True)
    expon = jnp.exp(scores - top_score)
    total = jnp.sum(expon, axis=-1, keepdims=True)
    weights = (expon / total).astype(jnp.bfloat16)
    mixed = jnp.einsum(
        "hqk,khd->qhd", weights, values_all.reshape(-1, H, HD), preferred_element_type=jnp.float32
    )
    return (mixed.reshape(queries.shape[0], H * HD), top_score[..., 0] + jnp.log(total[..., 0]))


def attend_backward(item):
    queries, keys_all, values_all, allowed, grad_mixed, log_total = item
    scores = score_block(queries, keys_all, allowed)
    probs = jnp.exp(scores - log_total[:, :, None])
    weights = probs.astype(jnp.bfloat16)
    grad_heads = grad_mixed.reshape(-1, H, HD)
    key_heads = keys_all.reshape(-1, H, HD)
    grad_weights = jnp.einsum(
        "qhd,khd->hqk",
        grad_heads,
        values_all.reshape(-1, H, HD),
        preferred_element_type=jnp.float32,
    )
    inner = jnp.sum(probs * grad_weights, axis=-1, keepdims=True)
    grad_scores = (probs * (grad_weights - inner)).astype(jnp.bfloat16)
    grad_query = jnp.einsum(
        "hqk,khd->qhd", grad_scores, key_heads, preferred_element_type=jnp.float32
    ) * HD ** (-0.5)
    grad_key = jnp.einsum(
        "hqk,qhd->khd", grad_scores, queries.reshape(-1, H, HD), preferred_element_type=jnp.float32
    ) * HD ** (-0.5)
    grad_value = jnp.einsum("hqk,qhd->khd", weights, grad_heads, preferred_element_type=jnp.float32)
    return (
        grad_query.reshape(queries.shape[0], H * HD),
        grad_key.reshape(keys_all.shape[0], H * HD),
        grad_value.reshape(keys_all.shape[0], H * HD),
    )


def on_device(
    inputs,
    segment_ids,
    cotangent,
    ln1_gain,
    ln1_bias,
    w_qkv,
    q_bias,
    v_bias,
    w_proj,
    proj_bias,
    ln2_gain,
    ln2_bias,
    w_fc,
    fc_bias,
    w_out,
    out_bias,
):
    width = inputs.shape[2]
    local_len = inputs.shape[1]
    per_batch = inputs.shape[0] // MICRO
    rank = lax.axis_index("fsdp")
    full_len = local_len * lax.axis_size("fsdp")
    key_segments = lax.all_gather(segment_ids, "fsdp", axis=1, tiled=True)
    query_pos = rank * local_len + jnp.arange(local_len)
    key_pos = jnp.arange(full_len)
    causal = key_pos[None, :] <= query_pos[:, None]
    allowed_all = (segment_ids[:, :, None] == key_segments[:, None, :]) & causal[None]
    shard_count = lax.axis_size(("dp", "fsdp"))
    totals = [
        jnp.zeros((piece.shape[0] * shard_count,) + piece.shape[1:], jnp.float32)
        for piece in (
            ln1_gain,
            ln1_bias,
            w_qkv,
            q_bias,
            v_bias,
            w_proj,
            proj_bias,
            ln2_gain,
            ln2_bias,
            w_fc,
            fc_bias,
            w_out,
            out_bias,
        )
    ]
    outputs_list = []
    grads_list = []
    for batch_index in range(MICRO):
        low_row = batch_index * per_batch
        high_row = low_row + per_batch
        gathered = (
            lax.all_gather(ln1_gain, ("dp", "fsdp"), axis=0, tiled=True),
            lax.all_gather(ln1_bias, ("dp", "fsdp"), axis=0, tiled=True),
            lax.all_gather(w_qkv, ("dp", "fsdp"), axis=0, tiled=True),
            lax.all_gather(q_bias, ("dp", "fsdp"), axis=0, tiled=True),
            lax.all_gather(v_bias, ("dp", "fsdp"), axis=0, tiled=True),
            lax.all_gather(w_proj, ("dp", "fsdp"), axis=0, tiled=True),
            lax.all_gather(proj_bias, ("dp", "fsdp"), axis=0, tiled=True),
            lax.all_gather(ln2_gain, ("dp", "fsdp"), axis=0, tiled=True),
            lax.all_gather(ln2_bias, ("dp", "fsdp"), axis=0, tiled=True),
            lax.all_gather(w_fc, ("dp", "fsdp"), axis=0, tiled=True),
            lax.all_gather(fc_bias, ("dp", "fsdp"), axis=0, tiled=True),
            lax.all_gather(w_out, ("dp", "fsdp"), axis=0, tiled=True),
            lax.all_gather(out_bias, ("dp", "fsdp"), axis=0, tiled=True),
        )
        (
            gain_first,
            shift_first,
            qkv_full,
            query_shift,
            value_shift,
            proj_full,
            proj_shift,
            gain_second,
            shift_second,
            expand_full,
            expand_shift,
            shrink_full,
            shrink_shift,
        ) = gathered
        tokens_in = inputs[low_row:high_row].astype(jnp.float32).reshape(-1, width)
        allowed = allowed_all[low_row:high_row]
        normed_low = layer_norm(tokens_in, gain_first, shift_first).astype(jnp.bfloat16)
        bias_all = jnp.concatenate([query_shift, jnp.zeros_like(query_shift), value_shift]).astype(
            jnp.float32
        )
        projected = (
            (row_dot(normed_low, qkv_full) + bias_all)
            .astype(jnp.bfloat16)
            .reshape(per_batch, local_len, 3 * width)
        )
        queries = projected[:, :, :width]
        own_keys = projected[:, :, width : 2 * width]
        own_values = projected[:, :, 2 * width :]
        keys_all, values_all = (
            lax.all_gather(own_keys, "fsdp", axis=1, tiled=True),
            lax.all_gather(own_values, "fsdp", axis=1, tiled=True),
        )
        mixed, log_total = lax.map(attend_forward, (queries, keys_all, values_all, allowed))
        mixed_low = mixed.astype(jnp.bfloat16).reshape(-1, width)
        middle = tokens_in + row_dot(mixed_low, proj_full) + proj_shift.astype(jnp.float32)
        normed_two_low = layer_norm(middle, gain_second, shift_second).astype(jnp.bfloat16)
        hidden = row_dot(normed_two_low, expand_full) + expand_shift.astype(jnp.float32)
        active_low = gelu_tanh(hidden).astype(jnp.bfloat16)
        result = middle + row_dot(active_low, shrink_full) + shrink_shift.astype(jnp.float32)
        outputs_list.append(result.astype(jnp.bfloat16).reshape(per_batch, local_len, width))
        (
            gain_first,
            shift_first,
            qkv_full,
            query_shift,
            value_shift,
            proj_full,
            proj_shift,
            gain_second,
            shift_second,
            expand_full,
            expand_shift,
            shrink_full,
            shrink_shift,
        ) = (
            lax.all_gather(ln1_gain, ("dp", "fsdp"), axis=0, tiled=True),
            lax.all_gather(ln1_bias, ("dp", "fsdp"), axis=0, tiled=True),
            lax.all_gather(w_qkv, ("dp", "fsdp"), axis=0, tiled=True),
            lax.all_gather(q_bias, ("dp", "fsdp"), axis=0, tiled=True),
            lax.all_gather(v_bias, ("dp", "fsdp"), axis=0, tiled=True),
            lax.all_gather(w_proj, ("dp", "fsdp"), axis=0, tiled=True),
            lax.all_gather(proj_bias, ("dp", "fsdp"), axis=0, tiled=True),
            lax.all_gather(ln2_gain, ("dp", "fsdp"), axis=0, tiled=True),
            lax.all_gather(ln2_bias, ("dp", "fsdp"), axis=0, tiled=True),
            lax.all_gather(w_fc, ("dp", "fsdp"), axis=0, tiled=True),
            lax.all_gather(fc_bias, ("dp", "fsdp"), axis=0, tiled=True),
            lax.all_gather(w_out, ("dp", "fsdp"), axis=0, tiled=True),
            lax.all_gather(out_bias, ("dp", "fsdp"), axis=0, tiled=True),
        )
        grad_out = cotangent[low_row:high_row].astype(jnp.float32).reshape(-1, width)
        grad_branch = grad_out.astype(jnp.bfloat16)
        totals[12] = totals[12] + jnp.sum(grad_branch.astype(jnp.float32), axis=0)
        totals[11] = totals[11] + col_dot(active_low, grad_branch)
        grad_active = back_dot(grad_branch, shrink_full)
        _, gelu_back = jax.vjp(gelu_tanh, hidden)
        grad_hidden = gelu_back(grad_active)[0].astype(jnp.bfloat16)
        totals[10] = totals[10] + jnp.sum(grad_hidden.astype(jnp.float32), axis=0)
        totals[9] = totals[9] + col_dot(normed_two_low, grad_hidden)
        grad_normed_two = back_dot(grad_hidden, expand_full)
        _, second_back = jax.vjp(
            layer_norm, middle, gain_second.astype(jnp.float32), shift_second.astype(jnp.float32)
        )
        grad_mid_part, grad_gain_two, grad_shift_two = second_back(grad_normed_two)
        totals[7] = totals[7] + grad_gain_two
        totals[8] = totals[8] + grad_shift_two
        grad_middle = grad_out + grad_mid_part
        grad_mid_low = grad_middle.astype(jnp.bfloat16)
        totals[6] = totals[6] + jnp.sum(grad_mid_low.astype(jnp.float32), axis=0)
        totals[5] = totals[5] + col_dot(mixed_low, grad_mid_low)
        grad_mixed = (
            back_dot(grad_mid_low, proj_full)
            .astype(jnp.bfloat16)
            .reshape(per_batch, local_len, width)
        )
        keys_back, values_back = (
            lax.all_gather(own_keys, "fsdp", axis=1, tiled=True),
            lax.all_gather(own_values, "fsdp", axis=1, tiled=True),
        )
        grad_query, key_terms, value_terms = lax.map(
            attend_backward, (queries, keys_back, values_back, allowed, grad_mixed, log_total)
        )
        grad_key, grad_value = (
            lax.psum_scatter(
                key_terms.astype(jnp.bfloat16), "fsdp", scatter_dimension=1, tiled=True
            ).astype(jnp.float32),
            lax.psum_scatter(
                value_terms.astype(jnp.bfloat16), "fsdp", scatter_dimension=1, tiled=True
            ).astype(jnp.float32),
        )
        grad_projected = (
            jnp.concatenate([grad_query, grad_key, grad_value], axis=-1)
            .astype(jnp.bfloat16)
            .reshape(-1, 3 * width)
        )
        totals[3] = totals[3] + jnp.sum(grad_projected[:, :width].astype(jnp.float32), axis=0)
        totals[4] = totals[4] + jnp.sum(grad_projected[:, 2 * width :].astype(jnp.float32), axis=0)
        totals[2] = totals[2] + col_dot(normed_low, grad_projected)
        grad_normed = back_dot(grad_projected, qkv_full)
        _, first_back = jax.vjp(
            layer_norm, tokens_in, gain_first.astype(jnp.float32), shift_first.astype(jnp.float32)
        )
        grad_in_part, grad_gain_one, grad_shift_one = first_back(grad_normed)
        totals[0] = totals[0] + grad_gain_one
        totals[1] = totals[1] + grad_shift_one
        grads_list.append(
            (grad_middle + grad_in_part).astype(jnp.bfloat16).reshape(per_batch, local_len, width)
        )
    owned = (
        lax.psum_scatter(totals[0], ("dp", "fsdp"), scatter_dimension=0, tiled=True),
        lax.psum_scatter(totals[1], ("dp", "fsdp"), scatter_dimension=0, tiled=True),
        lax.psum_scatter(totals[2], ("dp", "fsdp"), scatter_dimension=0, tiled=True),
        lax.psum_scatter(totals[3], ("dp", "fsdp"), scatter_dimension=0, tiled=True),
        lax.psum_scatter(totals[4], ("dp", "fsdp"), scatter_dimension=0, tiled=True),
        lax.psum_scatter(totals[5], ("dp", "fsdp"), scatter_dimension=0, tiled=True),
        lax.psum_scatter(totals[6], ("dp", "fsdp"), scatter_dimension=0, tiled=True),
        lax.psum_scatter(totals[7], ("dp", "fsdp"), scatter_dimension=0, tiled=True),
        lax.psum_scatter(totals[8], ("dp", "fsdp"), scatter_dimension=0, tiled=True),
        lax.psum_scatter(totals[9], ("dp", "fsdp"), scatter_dimension=0, tiled=True),
        lax.psum_scatter(totals[10], ("dp", "fsdp"), scatter_dimension=0, tiled=True),
        lax.psum_scatter(totals[11], ("dp", "fsdp"), scatter_dimension=0, tiled=True),
        lax.psum_scatter(totals[12], ("dp", "fsdp"), scatter_dimension=0, tiled=True),
    )
    return (
        jnp.concatenate(outputs_list, axis=0),
        jnp.concatenate(grads_list, axis=0),
        owned[0],
        owned[1],
        owned[2],
        owned[3],
        owned[4],
        owned[5],
        owned[6],
        owned[7],
        owned[8],
        owned[9],
        owned[10],
        owned[11],
        owned[12],
    )


def solution(mesh):
    placed = (
        P("dp", "fsdp", None),
        P("dp", "fsdp"),
        P("dp", "fsdp", None),
        P(("dp", "fsdp")),
        P(("dp", "fsdp")),
        P(("dp", "fsdp"), None),
        P(("dp", "fsdp")),
        P(("dp", "fsdp")),
        P(("dp", "fsdp"), None),
        P(("dp", "fsdp")),
        P(("dp", "fsdp")),
        P(("dp", "fsdp")),
        P(("dp", "fsdp"), None),
        P(("dp", "fsdp")),
        P(("dp", "fsdp"), None),
        P(("dp", "fsdp")),
    )
    return jax.shard_map(
        on_device,
        mesh=mesh,
        in_specs=placed,
        out_specs=(
            P("dp", "fsdp", None),
            P("dp", "fsdp", None),
            P(("dp", "fsdp")),
            P(("dp", "fsdp")),
            P(("dp", "fsdp"), None),
            P(("dp", "fsdp")),
            P(("dp", "fsdp")),
            P(("dp", "fsdp"), None),
            P(("dp", "fsdp")),
            P(("dp", "fsdp")),
            P(("dp", "fsdp")),
            P(("dp", "fsdp"), None),
            P(("dp", "fsdp")),
            P(("dp", "fsdp"), None),
            P(("dp", "fsdp")),
        ),
        check_vma=False,
    )
```

profile of v0, /device:TPU:0, one launch (start us, length us, event | category | flops | bytes accessed | tf_op | source)
XLA Modules:
  0.0 1259.6 jit_solution(14727537352222161990)
XLA Ops:
  14.7 42.6 %all-reduce.18 = (bf16[1024]{0:T(1024)(128)(2,1)S(1)}, bf16[1024]{0:T(1024)(128)(2,1)S(1)}, bf16[1024]{0:T(1024)(128)(2,1)S(1)}, bf16[1024]{0:T(1024)(128)(2,1)S...) all-reduce(bf16[1024]{0:T(1024)(128)(2,1)S(1)} %dynamic-update-slic, ...), channel_id=1, replica_groups=mesh['dp'=8,'fsdp'=4] {'dp','fsdp'}, use_global_device_ids=true, to_apply=%add.3 | all-reduce | flops 8192 | bytes 32768
  60.8 22.6 %all-gather.10.cloned.1.call-done = bf16[1024,3072]{1,0:T(8,128)(2,1)} async-done(((bf16[32,3072]{1,0:T(8,128)(2,1)}), bf16[1024,3072]{1,0:T(8,128)(2,1)}) %all-gather.10.cloned.1.call-update) | async-done | bytes 6291472 | tf_op jit(solution)/shard_map/all_gather | solution.py:144
  98.9 38.8 %all-gather = bf16[32,1,128]{2,1,0:T(2,128)(2,1)S(1)} all-gather(bf16[1,1,128]{2,1,0:T(2,128)(2,1)S(1)} %bitcast.242), channel_id=1, replica_groups=mesh['dp'=8,'fsdp'=4] {'dp','fsdp'}, dimensions={0}, use_global_device_ids=true | all-gather | bytes 8448 | tf_op jit(solution)/shard_map/all_gather | solution.py:152
  164.1 20.6 %all-gather.14.cloned.1.call-done = bf16[1,1024,1024]{2,1,0:T(8,128)(2,1)} async-done(((bf16[1,256,1024]{2,1,0:T(8,128)(2,1)}), bf16[1,1024,1024]{2,1,0:T(8,128)(2,1)}) %all-gather.14.cloned.1.call-update) | async-done | bytes 2097168 | tf_op jit(solution)/shard_map/all_gather | solution.py:186
  203.5 40.4 %all-gather.16.cloned.1.call-done = bf16[1024,1024]{1,0:T(8,128)(2,1)} async-done(((bf16[32,1024]{1,0:T(8,128)(2,1)}), bf16[1024,1024]{1,0:T(8,128)(2,1)}) %all-gather.16.cloned.1.call-update) | async-done | bytes 2097168 | tf_op jit(solution)/shard_map/all_gather | solution.py:147
  262.2 61.0 %all-gather.18.cloned.1.call-done = bf16[1024,4096]{1,0:T(8,128)(2,1)} async-done(((bf16[32,4096]{1,0:T(8,128)(2,1)}), bf16[1024,4096]{1,0:T(8,128)(2,1)}) %all-gather.18.cloned.1.call-update) | async-done | bytes 8388624 | tf_op jit(solution)/shard_map/all_gather | solution.py:151
  323.2 8.0 convolution_add_fusion.3
  335.7 66.6 %all-gather.20.cloned.1.call-done = bf16[4096,1024]{1,0:T(8,128)(2,1)} async-done(((bf16[128,1024]{1,0:T(8,128)(2,1)}), bf16[4096,1024]{1,0:T(8,128)(2,1)}) %all-gather.20.cloned.1.call-update) | async-done | bytes 8388624 | tf_op jit(solution)/shard_map/all_gather | solution.py:153
  402.2 8.3 convert_reduce_fusion
  410.6 6.5 fusion.119
  424.4 7.9 multiply_reduce_fusion.3
  437.1 9.2 fusion.30
  446.3 10.9 multiply_reduce_fusion.1
  457.2 8.0 multiply_convert_fusion.1
  473.5 9.3 fusion.33
  482.9 10.7 multiply_reduce_fusion
  493.6 8.1 multiply_convert_fusion
  511.2 7.0 fusion.53
  518.3 6.6 fusion.52
  525.0 7.9 fusion.75
  532.9 11.6 reduce-scatter.15.cloned.1.call-done
  544.5 34.0 %reduce-scatter.13.cloned.1.call-done = bf16[1,256,1024]{1,2,0:T(8,128)(2,1)} async-done(((bf16[1,1024,1024]{1,2,0:T(8,128)(2,1)}), bf16[1,256,1024]{1,2,0:T(8,128)(2,1)}) %reduce-scatter.13.cloned.1.call-update) | async-done | bytes 524304 | tf_op jit(solution)/shard_map/reduce_scatter | solution.py:259
  578.5 11.4 convolution_add_fusion.2
  595.0 10.1 convolution_add_fusion.1
  605.2 11.0 fusion.84
  616.2 11.2 convolution_add_fusion
  632.5 7.6 fusion.56
  653.5 40.7 %all-reduce.17 = (f32[1024]{0:T(1024)S(1)}, f32[1024]{0:T(1024)S(1)}, f32[1024]{0:T(1024)S(1)}, f32[1024]{0:T(1024)S(1)}, f32[1024]{0:T(1024)S(1)}, /*index=5*/f...) all-reduce(f32[1024]{0:T(1024)S(1)} %add.307, ...), channel_id=6, replica_groups=mesh['dp'=8,'fsdp'=4] {'dp','fsdp'}, use_global_device_ids=true, to_apply=%region_28.29.clone | all-reduce | flops 12288 | bytes 98304
  703.0 19.3 %reduce-scatter.19.cloned.1.call-done = f32[32,1024]{1,0:T(8,128)} async-done(((f32[1024,1024]{1,0:T(8,128)}), f32[32,1024]{1,0:T(8,128)}) %reduce-scatter.19.cloned.1.call-update) | async-done | bytes 131088 | tf_op jit(solution)/shard_map/reduce_scatter | solution.py:290
  722.4 157.8 %reduce-scatter.17.cloned.1.call-done = f32[32,3072]{1,0:T(8,128)} async-done(((f32[1024,3072]{1,0:T(8,128)}), f32[32,3072]{1,0:T(8,128)}) %reduce-scatter.17.cloned.1.call-update) | async-done | bytes 393232 | tf_op jit(solution)/shard_map/reduce_scatter | solution.py:287
  880.2 185.0 %reduce-scatter.21.cloned.1.call-done = f32[32,4096]{1,0:T(8,128)} async-done(((f32[1024,4096]{1,0:T(8,128)}), f32[32,4096]{1,0:T(8,128)}) %reduce-scatter.21.cloned.1.call-update) | async-done | bytes 524304 | tf_op jit(solution)/shard_map/reduce_scatter | solution.py:294
  1065.2 187.4 %reduce-scatter.23.cloned.1.call-done = f32[128,1024]{1,0:T(8,128)} async-done(((f32[4096,1024]{1,0:T(8,128)}), f32[128,1024]{1,0:T(8,128)}) %reduce-scatter.23.cloned.1.call-update) | async-done | bytes 524304 | tf_op jit(solution)/shard_map/reduce_scatter | solution.py:296
  (361 shorter events, 155.5 us)
Async XLA Ops:
  7.2 76.1 %all-gather.10.cloned.1.call-start = ((), (), s32[]{:S(2)}) async-start(), calls=%async_computation.8 | async-start | bytes 6488064 | tf_op jit(solution)/shard_map/all_gather | solution.py:144
  7.9 138.4 %all-gather.22.cloned.1.call-start = ((), (), s32[]{:S(2)}) async-start(), calls=%async_computation.14 | async-start | bytes 2621440 | tf_op jit(solution)/shard_map/all_gather | solution.py:187
  89.4 61.3 %all-gather.24.cloned.1.call-start = ((), (), s32[]{:S(2)}) async-start(), calls=%async_computation.15 | async-start | bytes 2621440 | tf_op jit(solution)/shard_map/all_gather | solution.py:186
  90.1 70.0 %all-gather.12.cloned.1.call-start = ((), (), s32[]{:S(2)}) async-start(), calls=%async_computation.9 | async-start | bytes 2621440 | tf_op jit(solution)/shard_map/all_gather | solution.py:187
  96.1 88.6 %all-gather.14.cloned.1.call-start = ((), (), s32[]{:S(2)}) async-start(), calls=%async_computation.10 | async-start | bytes 2621440 | tf_op jit(solution)/shard_map/all_gather | solution.py:186
  96.7 147.2 %all-gather.16.cloned.1.call-start = ((), (), s32[]{:S(2)}) async-start(), calls=%async_computation.11 | async-start | bytes 2162688 | tf_op jit(solution)/shard_map/all_gather | solution.py:147
  97.3 225.9 %all-gather.18.cloned.1.call-start = ((), (), s32[]{:S(2)}) async-start(), calls=%async_computation.12 | async-start | bytes 8650752 | tf_op jit(solution)/shard_map/all_gather | solution.py:151
  98.0 304.2 %all-gather.20.cloned.1.call-start = ((), (), s32[]{:S(2)}) async-start(), calls=%async_computation.13 | async-start | bytes 8650752 | tf_op jit(solution)/shard_map/all_gather | solution.py:153
  98.8 426.1 %reduce-scatter.11.cloned.1.call-start = ((), (), s32[]{:S(2)}) async-start(), calls=%async_computation.17 | async-start | bytes 2621440 | tf_op jit(solution)/shard_map/reduce_scatter | solution.py:262
  203.5 46.4 %copy-start.40 = (bf16[16,64,256]{2,1,0:T(8,128)(2,1)}, bf16[16,64,256]{2,1,0:T(8,128)(2,1)S(1)}, u32[]{:S(2)}) copy-start(bf16[16,64,256]{2,1,0:T(8,128)(2,1)S(1)} %fusion.54) | copy-start | bytes 1572868
  203.5 43.2 %copy-start.25 = (bf16[1,256,1024]{1,2,0:T(8,128)(2,1)S(1)}, bf16[1,256,1024]{1,2,0:T(8,128)(2,1)}, u32[]{:S(2)}) copy-start(bf16[1,256,1024]{1,2,0:T(8,128)(2,1)} %copy.56) | copy-start | bytes 1572868
  246.4 185.9 %copy-start.5 = (f32[256,1024]{1,0:T(8,128)}, f32[256,1024]{1,0:T(8,128)S(1)}, u32[]{:S(2)}) copy-start(f32[256,1024]{1,0:T(8,128)S(1)} %get-tuple-element.186) | copy-start | bytes 3145732
  246.5 185.9 %copy-start.72 = (f32[256]{0:T(256)}, f32[256]{0:T(256)S(1)}, u32[]{:S(2)}) copy-start(f32[256]{0:T(256)S(1)} %broadcast_multiply_fusion) | copy-start | bytes 3076
  261.9 170.5 %copy-start.11 = (f32[256,1024]{1,0:T(8,128)}, f32[256,1024]{1,0:T(8,128)S(1)}, u32[]{:S(2)}) copy-start(f32[256,1024]{1,0:T(8,128)S(1)} %get-tuple-element.190) | copy-start | bytes 3145732
  261.9 170.5 %copy-start.67 = (f32[256]{0:T(256)}, f32[256]{0:T(256)S(1)}, u32[]{:S(2)}) copy-start(f32[256]{0:T(256)S(1)} %broadcast_multiply_fusion.2) | copy-start | bytes 3076
  262.2 170.2 %copy-start.85 = (f32[256]{0:T(256)}, f32[256]{0:T(256)S(1)}, u32[]{:S(2)}) copy-start(f32[256]{0:T(256)S(1)} %fusion.97) | copy-start | bytes 3076
  262.2 170.2 %copy-start.73 = (f32[256]{0:T(256)}, f32[256]{0:T(256)S(1)}, u32[]{:S(2)}) copy-start(f32[256]{0:T(256)S(1)} %fusion.95) | copy-start | bytes 3076
  262.2 174.8 %copy-start.53 = (f32[16,256]{1,0:T(8,128)}, f32[16,256]{1,0:T(8,128)S(1)}, u32[]{:S(2)}) copy-start(f32[16,256]{1,0:T(8,128)S(1)} %log_add_fusion.1) | copy-start | bytes 49156
  446.3 78.7 %reduce-scatter.9.cloned.1.call-start = ((), (), s32[]{:S(2)}) async-start(), calls=%async_computation.16 | async-start | bytes 2621440 | tf_op jit(solution)/shard_map/reduce_scatter | solution.py:259
  469.5 75.0 %reduce-scatter.15.cloned.1.call-start = ((), (), s32[]{:S(2)}) async-start(), calls=%async_computation.19 | async-start | bytes 2621440 | tf_op jit(solution)/shard_map/reduce_scatter | solution.py:262
  482.8 95.7 %reduce-scatter.13.cloned.1.call-start = ((), (), s32[]{:S(2)}) async-start(), calls=%async_computation.18 | async-start | bytes 2621440 | tf_op jit(solution)/shard_map/reduce_scatter | solution.py:259
  505.6 216.8 %reduce-scatter.19.cloned.1.call-start = ((), (), s32[]{:S(2)}) async-start(), calls=%async_computation.21 | async-start | bytes 4325376 | tf_op jit(solution)/shard_map/reduce_scatter | solution.py:290
  509.6 370.6 %reduce-scatter.17.cloned.1.call-start = ((), (), s32[]{:S(2)}) async-start(), calls=%async_computation.20 | async-start | bytes 12976128 | tf_op jit(solution)/shard_map/reduce_scatter | solution.py:287
  525.0 53.5 %copy-start.31 = (bf16[16,64,256]{2,1,0:T(8,128)(2,1)S(1)}, bf16[16,64,256]{2,1,0:T(8,128)(2,1)}, u32[]{:S(2)}) copy-start(bf16[16,64,256]{2,1,0:T(8,128)(2,1)} %fusion.53) | copy-start | bytes 1572868
  525.0 53.5 %copy-start.63 = (f32[256]{0:T(256)S(1)}, f32[256]{0:T(256)}, u32[]{:S(2)}) copy-start(f32[256]{0:T(256)} %copy-done.62) | copy-start | bytes 3076
  525.0 53.5 %copy-start.70 = (f32[256]{0:T(256)S(1)}, f32[256]{0:T(256)}, u32[]{:S(2)}) copy-start(f32[256]{0:T(256)} %copy-done.69) | copy-start | bytes 3076
  590.0 475.2 %reduce-scatter.21.cloned.1.call-start = ((), (), s32[]{:S(2)}) async-start(), calls=%async_computation.22 | async-start | bytes 17301504 | tf_op jit(solution)/shard_map/reduce_scatter | solution.py:294
  605.1 647.5 %reduce-scatter.23.cloned.1.call-start = ((), (), s32[]{:S(2)}) async-start(), calls=%async_computation.23 | async-start | bytes 17301504 | tf_op jit(solution)/shard_map/reduce_scatter | solution.py:296
  651.8 47.7 %copy-start.16 = (bf16[2,256,1024]{2,1,0:T(8,128)(2,1)S(1)}, bf16[2,256,1024]{2,1,0:T(8,128)(2,1)}, u32[]{:S(2)}) copy-start(bf16[2,256,1024]{2,1,0:T(8,128)(2,1)} %param.18) | copy-start | bytes 3145732
  651.9 47.6 %copy-start.18 = (f32[256,1024]{1,0:T(8,128)S(1)}, f32[256,1024]{1,0:T(8,128)}, u32[]{:S(2)}) copy-start(f32[256,1024]{1,0:T(8,128)} %copy-done.17) | copy-start | bytes 3145732
  651.9 47.6 %copy-start.91 = (f32[256]{0:T(256)S(1)}, f32[256]{0:T(256)}, u32[]{:S(2)}) copy-start(f32[256]{0:T(256)} %copy-done.90) | copy-start | bytes 3076
  651.9 47.6 %copy-start.93 = (f32[256]{0:T(256)S(1)}, f32[256]{0:T(256)}, u32[]{:S(2)}) copy-start(f32[256]{0:T(256)} %copy-done.92) | copy-start | bytes 3076
  (90 other events, 659.7 us)
Sparse Core Ops, SparseCore 0:
  10.9 72.3 all-gather.9
  89.5 21.1 all-gather.21
  112.8 22.6 all-gather.23
  137.5 22.5 all-gather.11
  162.1 22.5 all-gather.13
  187.4 56.4 all-gather.15
  246.7 76.4 all-gather.17
  326.1 76.1 all-gather.19
  446.4 29.9 reduce-scatter.10
  478.9 31.4 reduce-scatter.8
  512.9 31.4 reduce-scatter.14
  547.0 31.4 reduce-scatter.12
  581.3 140.9 reduce-scatter.18
  728.8 151.3 reduce-scatter.16
  883.0 182.0 reduce-scatter.20
  1068.0 184.5 reduce-scatter.22
where the time goes:
time: 1270 us; the launch traced here: 1260 us
  waiting for transfers between devices  817 us (64%)
  matrix products  212 us (17%)
  blocking collectives  127 us (10%)
  local copies, waits for them, and re-layouts  45.4 us (4%)
  other arithmetic  41.2 us (3%)
  between operations  16 us (1%)
    reduce_scatter x1, waiting for transfers between devices, on_device(): lax.psum_scatter(totals[11], ('dp', 'fsdp'), scatter_dimension=0, tiled=T...  187 us
    reduce_scatter x1, waiting for transfers between devices, on_device(): lax.psum_scatter(totals[9], ('dp', 'fsdp'), scatter_dimension=0, tiled=True)  185 us
    reduce_scatter x1, waiting for transfers between devices, on_device(): lax.psum_scatter(totals[2], ('dp', 'fsdp'), scatter_dimension=0, tiled=True)  158 us
    unnamed x2, blocking collectives  83.3 us
    all_gather x1, waiting for transfers between devices, on_device(): lax.all_gather(w_out, ('dp', 'fsdp'), axis=0, tiled=True)  66.6 us
    all_gather x1, waiting for transfers between devices, on_device(): lax.all_gather(w_fc, ('dp', 'fsdp'), axis=0, tiled=True)  61 us
    dot_general x8, matrix products, col_dot(): lax.dot_general(left, right, (((0,), (0,)), ((), ())), preferred_element_...  59.6 us
    all_gather x1, waiting for transfers between devices, on_device(): lax.all_gather(w_proj, ('dp', 'fsdp'), axis=0, tiled=True)  40.4 us
  transfers between devices with their start and end apart: 16, of which 12 were waited for; matrix products, arithmetic and copies ran while one was open for 19% of the time, Pallas kernels for 0%

commit v1 on v0

v1 whole, which is shorter than its diff:
```python
import jax
import jax.numpy as jnp
from jax import lax
from jax.sharding import PartitionSpec as P

H = 16
HD = 64
PERMUTE = True


def layer_norm(values, gain, shift):
    center = values - jnp.mean(values, axis=-1, keepdims=True)
    spread = jnp.mean(center * center, axis=-1, keepdims=True)
    return center * lax.rsqrt(spread + 1e-05) * gain + shift


def gelu_tanh(values):
    return jax.nn.gelu(values, approximate=True)


def row_dot(left, right):
    return jnp.dot(left, right, preferred_element_type=jnp.float32)


def col_dot(left, right):
    return lax.dot_general(
        left, right, (((0,), (0,)), ((), ())), preferred_element_type=jnp.float32
    )


def back_dot(left, right):
    return lax.dot_general(
        left, right, (((1,), (1,)), ((), ())), preferred_element_type=jnp.float32
    )


def score_block(queries, keys_all, allowed):
    raw = jnp.einsum(
        "qhd,khd->hqk",
        queries.reshape(-1, H, HD),
        keys_all.reshape(-1, H, HD),
        preferred_element_type=jnp.float32,
    ) * HD ** (-0.5)
    return jnp.where(allowed[None], raw, -1e30)


def attend_forward(item):
    queries, keys_all, values_all, allowed = item
    scores = score_block(queries, keys_all, allowed)
    top_score = jnp.max(scores, axis=-1, keepdims=True)
    expon = jnp.exp(scores - top_score)
    total = jnp.sum(expon, axis=-1, keepdims=True)
    weights = (expon / total).astype(jnp.bfloat16)
    mixed = jnp.einsum(
        "hqk,khd->qhd", weights, values_all.reshape(-1, H, HD), preferred_element_type=jnp.float32
    )
    return (mixed.reshape(queries.shape[0], H * HD), top_score[..., 0] + jnp.log(total[..., 0]))


def attend_backward(item):
    queries, keys_all, values_all, allowed, grad_mixed, log_total = item
    scores = score_block(queries, keys_all, allowed)
    probs = jnp.exp(scores - log_total[:, :, None])
    weights = probs.astype(jnp.bfloat16)
    grad_heads = grad_mixed.reshape(-1, H, HD)
    key_heads = keys_all.reshape(-1, H, HD)
    grad_weights = jnp.einsum(
        "qhd,khd->hqk",
        grad_heads,
        values_all.reshape(-1, H, HD),
        preferred_element_type=jnp.float32,
    )
    inner = jnp.sum(probs * grad_weights, axis=-1, keepdims=True)
    grad_scores = (probs * (grad_weights - inner)).astype(jnp.bfloat16)
    grad_query = jnp.einsum(
        "hqk,khd->qhd", grad_scores, key_heads, preferred_element_type=jnp.float32
    ) * HD ** (-0.5)
    grad_key = jnp.einsum(
        "hqk,qhd->khd", grad_scores, queries.reshape(-1, H, HD), preferred_element_type=jnp.float32
    ) * HD ** (-0.5)
    grad_value = jnp.einsum("hqk,qhd->khd", weights, grad_heads, preferred_element_type=jnp.float32)
    return (
        grad_query.reshape(queries.shape[0], H * HD),
        grad_key.reshape(keys_all.shape[0], H * HD),
        grad_value.reshape(keys_all.shape[0], H * HD),
    )


def share_pack(segment_ids, vectors):
    batch, local_len = segment_ids.shape
    flat = jnp.concatenate([item for item in vectors] + [segment_ids.astype(jnp.bfloat16).reshape(-1)])
    rows = -(-flat.shape[0] // 2048) * 16
    flat = jnp.pad(flat, (0, rows * 128 - flat.shape[0])).reshape(rows, 128)
    everyone = lax.all_gather(flat, ("dp", "fsdp"), axis=0, tiled=True)
    everyone = everyone.reshape(-1, rows * 128)
    out = []
    low = 0
    for item in vectors:
        out.append(everyone[:, low : low + item.shape[0]].reshape(-1))
        low += item.shape[0]
    ranks = lax.axis_size("fsdp")
    mine = lax.dynamic_slice_in_dim(everyone, lax.axis_index("dp") * ranks, ranks, axis=0)
    mine = mine[:, low : low + batch * local_len].reshape(ranks, batch, local_len)
    key_segments = mine.transpose(1, 0, 2).reshape(batch, ranks * local_len).astype(jnp.int32)
    return out, key_segments


def scatter_pack(vectors):
    shards = lax.axis_size(("dp", "fsdp"))
    parts = [item.reshape(shards, -1) for item in vectors]
    flat = jnp.concatenate(parts, axis=1)
    rows = -(-flat.shape[1] // 1024) * 8
    flat = jnp.pad(flat, ((0, 0), (0, rows * 128 - flat.shape[1]))).reshape(shards * rows, 128)
    owned = lax.psum_scatter(flat, ("dp", "fsdp"), scatter_dimension=0, tiled=True).reshape(-1)
    out = []
    low = 0
    for item in parts:
        out.append(owned[low : low + item.shape[1]])
        low += item.shape[1]
    return out


def scatter_low(total):
    return lax.psum_scatter(
        total.astype(jnp.bfloat16), ("dp", "fsdp"), scatter_dimension=0, tiled=True
    ).astype(jnp.float32)


def share_keys(own):
    ranks = lax.axis_size("fsdp")
    if ranks != 4 or not PERMUTE:
        return lax.all_gather(own, "fsdp", axis=1, tiled=True)
    rank = lax.axis_index("fsdp")
    far = lax.ppermute(own, "fsdp", [(0, 2), (1, 3)])
    near = lax.ppermute(own, "fsdp", [(0, 1), (1, 0), (2, 3), (3, 2)])
    far_near = lax.ppermute(far, "fsdp", [(2, 3), (3, 2)])
    odd = (rank % 2) == 1
    high = rank >= 2
    pair = [jnp.where(odd, near, own), jnp.where(odd, own, near)]
    far_pair = [jnp.where(odd, far_near, far), jnp.where(odd, far, far_near)]
    empty = jnp.zeros_like(own)
    return jnp.concatenate(
        [
            jnp.where(high, far_pair[0], pair[0]),
            jnp.where(high, far_pair[1], pair[1]),
            jnp.where(high, pair[0], empty),
            jnp.where(high, pair[1], empty),
        ],
        axis=1,
    )


def return_keys(terms):
    ranks = lax.axis_size("fsdp")
    if ranks != 4 or not PERMUTE:
        return lax.psum_scatter(
            terms.astype(jnp.bfloat16), "fsdp", scatter_dimension=1, tiled=True
        ).astype(jnp.float32)
    rank = lax.axis_index("fsdp")
    part = terms.shape[1] // 4
    low_terms = terms.astype(jnp.bfloat16)
    odd = rank % 2
    other = 1 - odd
    base = (rank // 2) * 2
    pairs = [(0, 1), (1, 0), (2, 3), (3, 2)]

    def block(array, index):
        return lax.dynamic_slice_in_dim(array, index * part, part, axis=1)

    first = lax.ppermute(block(low_terms, other), "fsdp", [(2, 3), (3, 2)])
    far_sum = block(terms, odd) + first.astype(jnp.float32)
    near = lax.ppermute(block(low_terms, base + other), "fsdp", pairs)
    far = lax.ppermute(far_sum.astype(jnp.bfloat16), "fsdp", [(2, 0), (3, 1)])
    return block(terms, base + odd) + near.astype(jnp.float32) + far.astype(jnp.float32)


def on_device(
    inputs,
    segment_ids,
    cotangent,
    ln1_gain,
    ln1_bias,
    w_qkv,
    q_bias,
    v_bias,
    w_proj,
    proj_bias,
    ln2_gain,
    ln2_bias,
    w_fc,
    fc_bias,
    w_out,
    out_bias,
):
    batch, local_len, width = inputs.shape
    rank = lax.axis_index("fsdp")
    full_len = local_len * lax.axis_size("fsdp")
    small, key_segments = share_pack(
        segment_ids,
        (ln1_gain, ln1_bias, q_bias, v_bias, proj_bias, ln2_gain, ln2_bias, fc_bias, out_bias),
    )
    (
        gain_first,
        shift_first,
        query_shift,
        value_shift,
        proj_shift,
        gain_second,
        shift_second,
        expand_shift,
        shrink_shift,
    ) = [item.astype(jnp.float32) for item in small]
    qkv_full = lax.all_gather(w_qkv, ("dp", "fsdp"), axis=0, tiled=True)
    proj_full = lax.all_gather(w_proj, ("dp", "fsdp"), axis=0, tiled=True)
    expand_full = lax.all_gather(w_fc, ("dp", "fsdp"), axis=0, tiled=True)
    shrink_full = lax.all_gather(w_out, ("dp", "fsdp"), axis=0, tiled=True)
    query_pos = rank * local_len + jnp.arange(local_len)
    key_pos = jnp.arange(full_len)
    causal = key_pos[None, :] <= query_pos[:, None]
    allowed = (segment_ids[:, :, None] == key_segments[:, None, :]) & causal[None]

    tokens_in = inputs.astype(jnp.float32).reshape(-1, width)
    normed_low = layer_norm(tokens_in, gain_first, shift_first).astype(jnp.bfloat16)
    bias_all = jnp.concatenate([query_shift, jnp.zeros_like(query_shift), value_shift])
    projected = (
        (row_dot(normed_low, qkv_full) + bias_all)
        .astype(jnp.bfloat16)
        .reshape(batch, local_len, 3 * width)
    )
    queries = projected[:, :, :width]
    both_all = share_keys(projected[:, :, width:])
    keys_all = both_all[:, :, :width]
    values_all = both_all[:, :, width:]
    mixed, log_total = lax.map(attend_forward, (queries, keys_all, values_all, allowed))
    mixed_low = mixed.astype(jnp.bfloat16).reshape(-1, width)
    middle = tokens_in + row_dot(mixed_low, proj_full) + proj_shift
    normed_two_low = layer_norm(middle, gain_second, shift_second).astype(jnp.bfloat16)
    hidden = row_dot(normed_two_low, expand_full) + expand_shift
    active_low = gelu_tanh(hidden).astype(jnp.bfloat16)
    result = middle + row_dot(active_low, shrink_full) + shrink_shift
    block_output = result.astype(jnp.bfloat16).reshape(batch, local_len, width)

    grad_branch = cotangent.reshape(-1, width)
    grad_out = grad_branch.astype(jnp.float32)
    out_bias_grad = jnp.sum(grad_out, axis=0)
    w_out_grad = scatter_low(col_dot(active_low, grad_branch))
    grad_active = back_dot(grad_branch, shrink_full)
    _, gelu_back = jax.vjp(gelu_tanh, hidden)
    grad_hidden = gelu_back(grad_active)[0].astype(jnp.bfloat16)
    fc_bias_grad = jnp.sum(grad_hidden.astype(jnp.float32), axis=0)
    w_fc_grad = scatter_low(col_dot(normed_two_low, grad_hidden))
    grad_normed_two = back_dot(grad_hidden, expand_full)
    _, second_back = jax.vjp(layer_norm, middle, gain_second, shift_second)
    grad_mid_part, grad_gain_two, grad_shift_two = second_back(grad_normed_two)
    grad_middle = grad_out + grad_mid_part
    grad_mid_low = grad_middle.astype(jnp.bfloat16)
    proj_bias_grad = jnp.sum(grad_mid_low.astype(jnp.float32), axis=0)
    w_proj_grad = scatter_low(col_dot(mixed_low, grad_mid_low))
    grad_mixed = (
        back_dot(grad_mid_low, proj_full).astype(jnp.bfloat16).reshape(batch, local_len, width)
    )
    grad_query, key_terms, value_terms = lax.map(
        attend_backward, (queries, keys_all, values_all, allowed, grad_mixed, log_total)
    )
    grad_both = return_keys(jnp.concatenate([key_terms, value_terms], axis=-1))
    grad_projected = (
        jnp.concatenate([grad_query, grad_both], axis=-1)
        .astype(jnp.bfloat16)
        .reshape(-1, 3 * width)
    )
    q_bias_grad = jnp.sum(grad_projected[:, :width].astype(jnp.float32), axis=0)
    v_bias_grad = jnp.sum(grad_projected[:, 2 * width :].astype(jnp.float32), axis=0)
    w_qkv_grad = scatter_low(col_dot(normed_low, grad_projected))
    grad_normed = back_dot(grad_projected, qkv_full)
    _, first_back = jax.vjp(layer_norm, tokens_in, gain_first, shift_first)
    grad_in_part, grad_gain_one, grad_shift_one = first_back(grad_normed)
    input_grad = (grad_middle + grad_in_part).astype(jnp.bfloat16).reshape(batch, local_len, width)
    owned = scatter_pack(
        (
            grad_gain_one,
            grad_shift_one,
            q_bias_grad,
            v_bias_grad,
            proj_bias_grad,
            grad_gain_two,
            grad_shift_two,
            fc_bias_grad,
            out_bias_grad,
        )
    )
    return (
        block_output,
        input_grad,
        owned[0],
        owned[1],
        w_qkv_grad,
        owned[2],
        owned[3],
        w_proj_grad,
        owned[4],
        owned[5],
        owned[6],
        w_fc_grad,
        owned[7],
        w_out_grad,
        owned[8],
    )


def solution(mesh):
    placed = (
        P("dp", "fsdp", None),
        P("dp", "fsdp"),
        P("dp", "fsdp", None),
        P(("dp", "fsdp")),
        P(("dp", "fsdp")),
        P(("dp", "fsdp"), None),
        P(("dp", "fsdp")),
        P(("dp", "fsdp")),
        P(("dp", "fsdp"), None),
        P(("dp", "fsdp")),
        P(("dp", "fsdp")),
        P(("dp", "fsdp")),
        P(("dp", "fsdp"), None),
        P(("dp", "fsdp")),
        P(("dp", "fsdp"), None),
        P(("dp", "fsdp")),
    )
    return jax.shard_map(
        on_device,
        mesh=mesh,
        in_specs=placed,
        out_specs=(
            P("dp", "fsdp", None),
            P("dp", "fsdp", None),
            P(("dp", "fsdp")),
            P(("dp", "fsdp")),
            P(("dp", "fsdp"), None),
            P(("dp", "fsdp")),
            P(("dp", "fsdp")),
            P(("dp", "fsdp"), None),
            P(("dp", "fsdp")),
            P(("dp", "fsdp")),
            P(("dp", "fsdp")),
            P(("dp", "fsdp"), None),
            P(("dp", "fsdp")),
            P(("dp", "fsdp"), None),
            P(("dp", "fsdp")),
        ),
        check_vma=False,
    )
```

time: 1270 us -> 1200 us (0.945)
  blocking collectives: 127 us -> 44 us
  local copies, waits for them, and re-layouts: 45.4 us -> 110 us
  waiting for transfers between devices: 817 us -> 761 us
  matrix products: 212 us -> 182 us
  other arithmetic: 41.2 us -> 70.2 us
    reduce_scatter x8 -> x4, waiting for transfers between devices: 595 us -> 431 us  [scatter_low(): lax.psum_scatter(total.astype(jnp.bfloat16), ('dp', 'fsdp'), scatter_dime...]
    unnamed x16 -> x10, waiting for transfers between devices: 3.98 us -> 126 us
    all_gather x8 -> x4, waiting for transfers between devices: 218 us -> 100 us  [the longest x1 67 us: on_device(): shrink_full = lax.all_gather(w_out, ('dp', 'fsdp'), axis=0, tiled=True)]
    ppermute x0 -> x6, waiting for transfers between devices: none -> 103 us  [the longest x1 54.5 us: return_keys(): far = lax.ppermute(far_sum.astype(jnp.bfloat16), 'fsdp', [(2, 0), (3, 1)])]
    unnamed x2 -> x0, blocking collectives: 83.3 us -> none
    dynamic_update_slice x0 -> x14, local copies, waits for them, and re-layouts: none -> 44.9 us  [the longest x6 38.7 us: on_device(): lax.map(attend_backward, (queries, keys_all, values_all, allowed, grad_mi...]
    dot_general x2 -> x4, matrix products: 7.26 us -> 32.6 us  [score_block(): jnp.einsum('qhd,khd->hqk', queries.reshape(-1, H, HD), keys_all.reshape(-...]
    dot_general x8 -> x4, matrix products: 59.6 us -> 34.3 us  [col_dot(): lax.dot_general(left, right, (((0,), (0,)), ((), ())), preferred_element_...]
  transfers between devices with their start and end apart: 16 -> 15, of which waited for: 12 -> 10; matrix products, arithmetic and copies ran while one was open for 19% -> 14% of each run, Pallas kernels for 0% -> 0%
where the time goes in v1:
time: 1200 us; the launch traced here: 1190 us
  waiting for transfers between devices  761 us (63%)
  matrix products  182 us (15%)
  local copies, waits for them, and re-layouts  110 us (9%)
  other arithmetic  70.2 us (6%)
  blocking collectives  44 us (4%)
  between operations  14.7 us (1%)
    reduce_scatter x4, waiting for transfers between devices, scatter_low(): lax.psum_scatter(total.astype(jnp.bfloat16), ('dp', 'fsdp'), scatter_dime...  431 us
    unnamed x10, waiting for transfers between devices  126 us
    all_gather x1, waiting for transfers between devices, on_device(): shrink_full = lax.all_gather(w_out, ('dp', 'fsdp'), axis=0, tiled=True)  67 us
    ppermute x1, waiting for transfers between devices, return_keys(): far = lax.ppermute(far_sum.astype(jnp.bfloat16), 'fsdp', [(2, 0), (3, 1)])  54.5 us
    ppermute x1, waiting for transfers between devices, share_keys(): far = lax.ppermute(own, 'fsdp', [(0, 2), (1, 3)])  49 us
    all_gather x1, blocking collectives, share_pack(): everyone = lax.all_gather(flat, ('dp', 'fsdp'), axis=0, tiled=True)  44 us
    dynamic_update_slice x6, local copies, waits for them, and re-layouts, on_device(): lax.map(attend_backward, (queries, keys_all, values_all, allowed, grad_mi...  38.7 us
    dot_general x4, matrix products, row_dot(): return jnp.dot(left, right, preferred_element_type=jnp.float32)  34.5 us
  transfers between devices with their start and end apart: 15, of which 10 were waited for; matrix products, arithmetic and copies ran while one was open for 14% of the time, Pallas kernels for 0%

profile of v1, /device:TPU:0, one launch (start us, length us, event | category | flops | bytes accessed | tf_op | source)
XLA Modules:
  0.0 1194.5 jit_solution(6556213538068715534)
XLA Ops:
  13.8 6.1 concatenate.24
  19.9 44.0 %all_gather.15 = bf16[512,128]{1,0:T(8,128)(2,1)S(1)} all-gather(bf16[16,128]{1,0:T(8,128)(2,1)S(1)} %pad_bitcast_fusion), channel_id=1, replica_groups=mesh['dp'=8,'fsdp'=4] {'dp','fsdp'}, dimensions={0}, use_global_device_ids=true | all-gather | bytes 135168 | tf_op jit(solution)/shard_map/all_gather | solution.py:94
  66.7 16.7 %all-gather.5.cloned.1.call-done = bf16[1024,3072]{1,0:T(8,128)(2,1)} async-done(((bf16[32,3072]{1,0:T(8,128)(2,1)}), bf16[1024,3072]{1,0:T(8,128)(2,1)}) %all-gather.5.cloned.1.call-update) | async-done | bytes 6291472 | tf_op jit(solution)/shard_map/all_gather | solution.py:213
  83.4 6.4 add_convert_fusion
  98.8 49.0 %collective-permute-done = bf16[2,256,2048]{1,2,0:T(8,128)(2,1)} collective-permute-done((bf16[2,256,2048]{1,2,0:T(8,128)(2,1)}, bf16[2,256,2048]{1,2,0:T(8,128)(2,1)}, u32[]{:S(2)}, u32[]{:S(2)}) %collective-permute-start) | collective-permute-done | bytes 2097184 | tf_op jit(solution)/shard_map/ppermute | solution.py:134
  165.4 36.8 %while.26 = (s32[]{:T(128)}, bf16[2,256,1024]{2,1,0:T(8,128)(2,1)}, f32[2,16,256]{2,1,0:T(8,128)S(1)}, bf16[2,1024,1024]{1,2,0:T(8,128)(2,1)}, pred[2,256,1024]{...) while((s32[]{:T(128)}, bf16[2,256,1024]{2,1,0:T(8,128)(2,1)}, ...), condition=%wide.region_5.6_spmd, body=%wide.region_2.5_spmd.sunk | while | flops 1124069376 | bytes 68550760 | solution.py:234
  175.7 5.8 fusion.96
  193.8 5.8 fusion.96
  206.9 16.6 %all-gather.9.cloned.1.call-done = bf16[1024,4096]{1,0:T(8,128)(2,1)} async-done(((bf16[32,4096]{1,0:T(8,128)(2,1)}), bf16[1024,4096]{1,0:T(8,128)(2,1)}) %all-gather.9.cloned.1.call-update) | async-done | bytes 8388624 | tf_op jit(solution)/shard_map/all_gather | solution.py:215
  223.5 11.9 fusion.34
  235.3 67.0 %all-gather.11.cloned.1.call-done = bf16[4096,1024]{1,0:T(8,128)(2,1)} async-done(((bf16[128,1024]{1,0:T(8,128)(2,1)}), bf16[4096,1024]{1,0:T(8,128)(2,1)}) %all-gather.11.cloned.1.call-update) | async-done | bytes 8388624 | tf_op jit(solution)/shard_map/all_gather | solution.py:216
  302.4 13.8 %convert_reduce_fusion = (f32[4096]{0:T(1024)}, bf16[512,4096]{1,0:T(8,128)(2,1)S(1)}) fusion(f32[512,4096]{1,0:T(8,128)} %fusion.34, f32[4096]{0:T(1024)S(1)} %copy-done.43, bf16[512,1024]{1,0:T(8,128)(2,1)S(1)} %bitcast.191, bf16[4096,1024]{1,0:T(8,128)(2,1)} %all-gather.11.cloned.1.call-done), kind=kOutput, calls=%fused_computation.40 | convolution fusion | flops 4343197696 | bytes 22052864 | tf_op jit(solution)/shard_map/dot_general | solution.py:32
  326.1 148.2 %while.27 = (s32[]{:T(128)}, bf16[2,256,1024]{2,1,0:T(8,128)(2,1)}, f32[2,1024,1024]{2,1,0:T(8,128)}, f32[2,1024,1024]{2,1,0:T(8,128)}, bf16[2,1024,1024]{1,2,0:...) while((s32[]{:T(128)}, bf16[2,256,1024]{2,1,0:T(8,128)(2,1)}, ...), condition=%wide.region_12.13_spmd, body=%wide.region_10.12_spmd.sunk | while | flops 2723672064 | bytes 306528704 | solution.py:262
  330.7 8.1 fusion.107
  338.8 13.2 %multiply_reduce_fusion.5 = (f32[16,256]{1,0:T(8,128)S(1)}, f32[16,256,1024]{2,1,0:T(8,128)}) fusion(f32[16,256,1024]{2,1,0:T(8,128)} %fusion.107, f32[16,256]{1,0:T(8,128)S(1)} %dynamic-slice_bitcast_fusion.8, bf16[256,16,64]{0,2,1:T(8,128)(2,1)S(1)} %bitcast.183, bf16[1024,16,64]{0,2,1:T(8,128)(2,1)S(1)} %bitcast.178, ...), kind=kOutput, calls=%fused_computation.15.clone.1 | convolution fusion | flops 557838336 | bytes 36470784 | tf_op jit(solution)/shard_map/while/body/eval_jaxpr/qhd,khd->hqk/dot_general | solution.py:38
  352.0 11.5 multiply_convert_fusion.5
  391.7 8.6 constant_dynamic-update-slice_fusion.11
  404.6 8.1 fusion.107
  412.8 13.2 %multiply_reduce_fusion.5 = (f32[16,256]{1,0:T(8,128)S(1)}, f32[16,256,1024]{2,1,0:T(8,128)}) fusion(f32[16,256,1024]{2,1,0:T(8,128)} %fusion.107, f32[16,256]{1,0:T(8,128)S(1)} %dynamic-slice_bitcast_fusion.8, bf16[256,16,64]{0,2,1:T(8,128)(2,1)S(1)} %bitcast.183, bf16[1024,16,64]{0,2,1:T(8,128)(2,1)S(1)} %bitcast.178, ...), kind=kOutput, calls=%fused_computation.15.clone.1 | convolution fusion | flops 557838336 | bytes 36470784 | tf_op jit(solution)/shard_map/while/body/eval_jaxpr/qhd,khd->hqk/dot_general | solution.py:38
  426.0 11.5 multiply_convert_fusion.5
  465.7 8.5 constant_dynamic-update-slice_fusion.11
  503.9 54.5 %collective-permute-done.5 = bf16[2,256,2048]{2,1,0:T(8,128)(2,1)} collective-permute-done((bf16[2,256,2048]{2,1,0:T(8,128)(2,1)}, bf16[2,256,2048]{2,1,0:T(8,128)(2,1)}, u32[]{:S(2)}, u32[]{:S(2)}) %collective-permute-start.5) | collective-permute-done | bytes 2097184 | tf_op jit(solution)/shard_map/ppermute | solution.py:173
  563.1 7.5 fusion.35
  575.4 7.7 convolution_convert_fusion.2
  583.8 13.1 %convolution_convert_fusion = bf16[4096,1024]{1,0:T(8,128)(2,1)} fusion(bf16[512,1024]{1,0:T(8,128)(2,1)S(1)} %bitcast.192, f32[512,4096]{1,0:T(8,128)} %fusion.34, f32[4096]{0:T(1024)S(1)} %copy-done.44), kind=kOutput, calls=%fused_computation.42 | convolution fusion | flops 4320133120 | bytes 17842176 | tf_op jit(solution)/shard_map/dot_general | solution.py:26
  597.6 10.8 convolution_convert_fusion.1
  609.2 13.0 %add_convert_fusion.4 = bf16[512,1024]{1,0:T(8,128)(2,1)} fusion(f32[512,1024]{1,0:T(8,128)} %copy-done.17, bf16[4096,1024]{1,0:T(8,128)(2,1)} %all-gather.11.cloned.1.call-done, f32[1024]{0:T(1024)S(1)} %reshape.368, f32[512,4096]{1,0:T(8,128)} %fusion.34, f32[4096]{0:T(1024)S(1)} %copy-done.44), kind=kOutput, calls=%fused_computation.75 | convolution fusion | flops 4317511680 | bytes 19943424 | tf_op jit(solution)/shard_map/dot_general | solution.py:22
  624.3 18.6 %reduce-scatter.7.cloned.1.call-done = bf16[32,1024]{1,0:T(8,128)(2,1)} async-done(((bf16[1024,1024]{1,0:T(8,128)(2,1)}), bf16[32,1024]{1,0:T(8,128)(2,1)}) %reduce-scatter.7.cloned.1.call-update) | async-done | bytes 65552 | tf_op jit(solution)/shard_map/reduce_scatter | solution.py:124
  644.4 123.8 %all-reduce.5.cloned.1.call-done = f32[256,128]{1,0:T(8,128)} async-done(((f32[256,128]{1,0:T(8,128)}), f32[256,128]{1,0:T(8,128)}) %all-reduce.5.cloned.1.call-update) | async-done | bytes 131088
  770.0 118.1 %reduce-scatter.5.cloned.1.call-done = bf16[32,3072]{1,0:T(8,128)(2,1)} async-done(((bf16[1024,3072]{1,0:T(8,128)(2,1)}), bf16[32,3072]{1,0:T(8,128)(2,1)}) %reduce-scatter.5.cloned.1.call-update) | async-done | bytes 196624 | tf_op jit(solution)/shard_map/reduce_scatter | solution.py:124
  889.8 149.0 %reduce-scatter.11.cloned.1.call-done = bf16[128,1024]{1,0:T(8,128)(2,1)} async-done(((bf16[4096,1024]{1,0:T(8,128)(2,1)}), bf16[128,1024]{1,0:T(8,128)(2,1)}) %reduce-scatter.11.cloned.1.call-update) | async-done | bytes 262160 | tf_op jit(solution)/shard_map/reduce_scatter | solution.py:124
  1040.6 145.3 %reduce-scatter.9.cloned.1.call-done = bf16[32,4096]{1,0:T(8,128)(2,1)} async-done(((bf16[1024,4096]{1,0:T(8,128)(2,1)}), bf16[32,4096]{1,0:T(8,128)(2,1)}) %reduce-scatter.9.cloned.1.call-update) | async-done | bytes 262160 | tf_op jit(solution)/shard_map/reduce_scatter | solution.py:124
  (293 shorter events, 191.5 us)
Async XLA Ops:
  7.2 76.2 %all-gather.5.cloned.1.call-start = ((), (), s32[]{:S(2)}) async-start(), calls=%async_computation.4 | async-start | bytes 6488064 | tf_op jit(solution)/shard_map/all_gather | solution.py:213
  7.9 194.3 %all-gather.7.cloned.1.call-start = ((), (), s32[]{:S(2)}) async-start(), calls=%async_computation.5 | async-start | bytes 2162688 | tf_op jit(solution)/shard_map/all_gather | solution.py:214
  8.7 214.8 %all-gather.9.cloned.1.call-start = ((), (), s32[]{:S(2)}) async-start(), calls=%async_computation.6 | async-start | bytes 8650752 | tf_op jit(solution)/shard_map/all_gather | solution.py:215
  9.4 293.0 %all-gather.11.cloned.1.call-start = ((), (), s32[]{:S(2)}) async-start(), calls=%async_computation.7 | async-start | bytes 8650752 | tf_op jit(solution)/shard_map/all_gather | solution.py:216
  11.6 78.2 %copy-start.31 = (f32[1,2,2,128]{3,1,2,0:T(2,128)}, f32[1,2,2,128]{3,1,2,0:T(2,128)S(1)}, u32[]{:S(2)}) copy-start(f32[1,2,2,128]{3,1,2,0:T(2,128)S(1)} %copy.77) | copy-start | bytes 6148
  13.8 76.0 %copy-start.33 = (f32[512]{0:T(512)}, f32[512]{0:T(512)S(1)}, u32[]{:S(2)}) copy-start(f32[512]{0:T(512)S(1)} %rsqrt.22) | copy-start | bytes 6148
  64.8 25.0 %copy-start.28 = (f32[1024]{0:T(1024)}, f32[1024]{0:T(1024)S(1)}, u32[]{:S(2)}) copy-start(f32[1024]{0:T(1024)S(1)} %reshape.359) | copy-start | bytes 12292
  66.7 23.1 %copy-start.25 = (bf16[512,1024]{1,0:T(8,128)(2,1)}, bf16[512,1024]{1,0:T(8,128)(2,1)S(1)}, u32[]{:S(2)}) copy-start(bf16[512,1024]{1,0:T(8,128)(2,1)S(1)} %fusion.20) | copy-start | bytes 3145732
  91.4 61.7 %copy-start.47 = (s32[2,256]{1,0:T(2,128)S(1)}, s32[2,256]{1,0:T(2,128)}, u32[]{:S(2)}) copy-start(s32[2,256]{1,0:T(2,128)} %param.21) | copy-start | bytes 6148
  94.1 53.6 %collective-permute-start = (bf16[2,256,2048]{1,2,0:T(8,128)(2,1)}, bf16[2,256,2048]{1,2,0:T(8,128)(2,1)}, u32[]{:S(2)}, u32[]{:S(2)}) collective-permute-start(bf16[2,256,2048]{1,2,0:T(8,128)(2,1)} %copy.57), channel_id=1, source_target_pairs={{0,2},{1,3},{4,6},{5,7},{8,10},{9,11},{12,14},{13,15},{16,18},{17,... | collective-permute-start | bytes 6291464 | tf_op jit(solution)/shard_map/ppermute | solution.py:134
  98.8 56.6 %collective-permute-start.2 = (bf16[2,256,2048]{1,2,0:T(8,128)(2,1)}, bf16[2,256,2048]{1,2,0:T(8,128)(2,1)}, u32[]{:S(2)}, u32[]{:S(2)}) collective-permute-start(bf16[2,256,2048]{1,2,0:T(8,128)(2,1)} %copy.57), channel_id=1, source_target_pairs={{0,1},{1,0},{2,3},{3,2},{4,5},{5,4},{6,7},{7,6},{8,9},{9,8},{10,11... | collective-permute-start | bytes 6291464 | tf_op jit(solution)/shard_map/ppermute | solution.py:135
  147.8 7.7 collective-permute-start.1
  149.8 493.1 %reduce-scatter.7.cloned.1.call-start = ((), (), s32[]{:S(2)}) async-start(), calls=%async_computation.9 | async-start | bytes 2162688 | tf_op jit(solution)/shard_map/reduce_scatter | solution.py:124
  165.3 36.9 %copy-start.7 = (bf16[2,256,1024]{2,1,0:T(8,128)(2,1)S(1)}, bf16[2,256,1024]{2,1,0:T(8,128)(2,1)}, u32[]{:S(2)}) copy-start(bf16[2,256,1024]{2,1,0:T(8,128)(2,1)} %param.20) | copy-start | bytes 3145732
  165.3 36.9 %copy-start.54 = (f32[1024]{0:T(1024)S(1)}, f32[1024]{0:T(1024)}, u32[]{:S(2)}) copy-start(f32[1024]{0:T(1024)} %reshape.364) | copy-start | bytes 12292
  202.2 21.3 %copy-start.45 = (f32[1024]{0:T(1024)S(1)}, f32[1024]{0:T(1024)}, u32[]{:S(2)}) copy-start(f32[1024]{0:T(1024)} %reshape.365) | copy-start | bytes 12292
  202.2 21.3 %copy-start.50 = (f32[1024]{0:T(1024)S(1)}, f32[1024]{0:T(1024)}, u32[]{:S(2)}) copy-start(f32[1024]{0:T(1024)} %reshape.366) | copy-start | bytes 12292
  205.5 116.2 %copy-start.39 = (f32[512]{0:T(512)}, f32[512]{0:T(512)S(1)}, u32[]{:S(2)}) copy-start(f32[512]{0:T(512)S(1)} %broadcast_multiply_fusion) | copy-start | bytes 6148
  206.9 114.8 %copy-start.48 = (f32[512]{0:T(512)}, f32[512]{0:T(512)S(1)}, u32[]{:S(2)}) copy-start(f32[512]{0:T(512)S(1)} %fusion.29) | copy-start | bytes 6148
  206.9 95.5 %copy-start.13 = (bf16[2,256,1024]{2,1,0:T(8,128)(2,1)S(1)}, bf16[2,256,1024]{2,1,0:T(8,128)(2,1)}, u32[]{:S(2)}) copy-start(bf16[2,256,1024]{2,1,0:T(8,128)(2,1)} %param.22) | copy-start | bytes 3145732
  206.9 95.5 %copy-start.43 = (f32[4096]{0:T(1024)S(1)}, f32[4096]{0:T(1024)}, u32[]{:S(2)}) copy-start(f32[4096]{0:T(1024)} %fusion.28) | copy-start | bytes 49156
  426.0 15.4 %copy-start = (f32[16,256,1024]{2,1,0:T(8,128)S(1)}, f32[16,256,1024]{2,1,0:T(8,128)}, u32[]{:S(2)}) copy-start(f32[16,256,1024]{2,1,0:T(8,128)} %get-tuple-element.343) | copy-start | bytes 50331652 | tf_op jit(solution)/shard_map/while
  490.4 2.3 collective-permute-start.4
  492.4 11.5 collective-permute-start.3
  497.7 60.7 %collective-permute-start.5 = (bf16[2,256,2048]{2,1,0:T(8,128)(2,1)}, bf16[2,256,2048]{2,1,0:T(8,128)(2,1)}, u32[]{:S(2)}, u32[]{:S(2)}) collective-permute-start(bf16[2,256,2048]{2,1,0:T(8,128)(2,1)} %add_convert_fusion.2), channel_id=1, source_target_pairs={{2,0},{3,1},{6,4},{7,5},{10,8},{11,9},{14,12},{15,13},{18,16},{19,... | collective-permute-start | bytes 6291464 | tf_op jit(solution)/shard_map/ppermute | solution.py:173
  501.8 266.3 %all-reduce.5.cloned.1.call-start = ((), (), s32[]{:S(2)}) async-start(), calls=%async_computation.12 | async-start | bytes 262144
  503.9 59.2 %copy-start.8 = (bf16[2,256,1024]{2,1,0:T(8,128)(2,1)S(1)}, bf16[2,256,1024]{2,1,0:T(8,128)(2,1)}, u32[]{:S(2)}) copy-start(bf16[2,256,1024]{2,1,0:T(8,128)(2,1)} %param.20) | copy-start | bytes 3145732
  503.9 59.2 %copy-start.29 = (f32[1024]{0:T(1024)S(1)}, f32[1024]{0:T(1024)}, u32[]{:S(2)}) copy-start(f32[1024]{0:T(1024)} %copy-done.28) | copy-start | bytes 12292
  503.9 59.2 %copy-start.32 = (f32[1,2,2,128]{3,1,2,0:T(2,128)S(1)}, f32[1,2,2,128]{3,1,2,0:T(2,128)}, u32[]{:S(2)}) copy-start(f32[1,2,2,128]{3,1,2,0:T(2,128)} %copy-done.31) | copy-start | bytes 6148
  575.3 312.8 %reduce-scatter.5.cloned.1.call-start = ((), (), s32[]{:S(2)}) async-start(), calls=%async_computation.8 | async-start | bytes 6488064 | tf_op jit(solution)/shard_map/reduce_scatter | solution.py:124
  583.1 455.7 %reduce-scatter.11.cloned.1.call-start = ((), (), s32[]{:S(2)}) async-start(), calls=%async_computation.11 | async-start | bytes 8650752 | tf_op jit(solution)/shard_map/reduce_scatter | solution.py:124
  596.9 589.0 %reduce-scatter.9.cloned.1.call-start = ((), (), s32[]{:S(2)}) async-start(), calls=%async_computation.10 | async-start | bytes 8650752 | tf_op jit(solution)/shard_map/reduce_scatter | solution.py:124
  (51 other events, 266.1 us)
Sparse Core Ops, SparseCore 0:
  10.9 72.4 all-gather.4
  86.2 55.1 all-gather.6
  144.3 79.1 all-gather.8
  226.2 76.1 all-gather.10
  502.0 140.8 reduce-scatter.6
  649.8 118.3 all-reduce.4
  774.7 113.3 reduce-scatter.4
  890.4 148.4 reduce-scatter.10
  1041.1 144.7 reduce-scatter.8
